TPU v7x, 32 devices: a whole 2x2x4 slice. The times are simulated.
32 devices in a mesh: groups: 2 (over y), seq: 4 (over z), tp: 4 (over x, core).
Axes of the slice: x: 2, y: 2, z: 4, core: 2. Of those that a mesh axis runs over, the one named last changes fastest.
Arguments:
- branches: bfloat16 [1024, 3, 2048], P(('groups', 'seq'), None, 'tp'), parts along dimension 0, may hold values from -5 to 5
- residual: bfloat16 [1024, 4096], P(('groups', 'seq'), 'tp'), parts along dimension 0, may hold values from -32 to 32
- segments: int32 [1024], P('groups'), parts along dimension 0, may hold values from 0 to 7, never falling along the last dimension, each value on 1 to 256 neighbouring positions
- long_filter: float32 [512, 2048], P('seq', 'tp'), may hold values from -4 to 4
- short_taps: float32 [3, 3, 2048], P(None, None, 'tp'), may hold values from -3 to 3
- skip_gain: float32 [2048], P('tp'), may hold values from -3 to 3
- out_weight: bfloat16 [2048, 4096], P(None, 'tp'), may hold values from -0.125 to 0.125
- norm_gain: float32 [4096], replicated, may hold values from 0.1 to 1.9
- head_weight: bfloat16 [4096, 3, 2048], P(None, None, 'tp'), may hold values from -27 to 27
Outputs:
- hidden: bfloat16 [1024, 4096], P(('groups', 'seq'), 'tp'), parts along dimension 0
- context: bfloat16 [1024, 2048], P(('groups', 'seq'), 'tp'), parts along dimension 0
There are 2 independent parts, one for each index of `groups`. A program takes and returns all parts, laid end to end along the dimension named above; an argument that names none is the same for every part. Nothing has to cross between parts.
Inputs may be any that keep to these rules, and one draw needn't show every extreme that they name: `segments`: document ids never fall along the window; a document holds 1 to 256 positions, and one holds exactly 256.
All inputs are finite; a program needn't handle non-finite values.
Results may differ from a plain program's by a relative error of at most 0.017.
Values may be sent and summed in bfloat16 or wider, within the bound.
A program may use at most 64 MiB of HBM per device.

v0:
```python
import math

import jax
import jax.numpy as jnp
from jax import lax
from jax.sharding import PartitionSpec as P

DH = 128


EPSILON = 1e-05
HIGHEST = lax.Precision.HIGHEST
TWO_PI = 2.0 * math.pi


def passed_along(array, axis, by):
    count = lax.axis_size(axis)
    pairs = [(i, i + by) for i in range(count) if 0 <= i + by < count]
    return lax.ppermute(array, axis, pairs)


def complex_times(left_real, left_imag, right_real, right_imag):
    return (
        left_real * right_real - left_imag * right_imag,
        left_real * right_imag + left_imag * right_real,
    )


def window_convolve(whole, shards):
    count = whole.shape[1]
    rows = count // shards
    span = 2 * shards
    total = 2 * count
    data = whole.reshape(2, shards, rows, whole.shape[2])
    outer_index = jnp.arange(span, dtype=jnp.int32)
    block_index = jnp.arange(shards, dtype=jnp.int32)
    place_index = jnp.arange(rows, dtype=jnp.int32)
    outer = TWO_PI * (outer_index[:, None] * block_index[None, :] % span).astype(jnp.float32) / span
    outer_cos = jnp.cos(outer)
    outer_sin = jnp.sin(outer)
    first_real = jnp.einsum("ka,sabc->skbc", outer_cos, data, precision=HIGHEST)
    first_imag = -jnp.einsum("ka,sabc->skbc", outer_sin, data, precision=HIGHEST)
    twist = (
        TWO_PI * (outer_index[:, None] * place_index[None, :] % total).astype(jnp.float32) / total
    )
    twist_cos = jnp.cos(twist)[:, :, None]
    twist_sin = jnp.sin(twist)[:, :, None]
    turned_real, turned_imag = complex_times(first_real, first_imag, twist_cos, -twist_sin)
    inner = TWO_PI * (place_index[:, None] * place_index[None, :] % rows).astype(jnp.float32) / rows
    inner_cos = jnp.cos(inner)
    inner_sin = jnp.sin(inner)
    spec_real = jnp.einsum("bq,skbc->skqc", inner_cos, turned_real, precision=HIGHEST) + jnp.einsum(
        "bq,skbc->skqc", inner_sin, turned_imag, precision=HIGHEST
    )
    spec_imag = jnp.einsum("bq,skbc->skqc", inner_cos, turned_imag, precision=HIGHEST) - jnp.einsum(
        "bq,skbc->skqc", inner_sin, turned_real, precision=HIGHEST
    )
    prod_real, prod_imag = complex_times(spec_real[0], spec_imag[0], spec_real[1], spec_imag[1])
    back_real = jnp.einsum("qb,kqc->kbc", inner_cos, prod_real, precision=HIGHEST) - jnp.einsum(
        "qb,kqc->kbc", inner_sin, prod_imag, precision=HIGHEST
    )
    back_imag = jnp.einsum("qb,kqc->kbc", inner_cos, prod_imag, precision=HIGHEST) + jnp.einsum(
        "qb,kqc->kbc", inner_sin, prod_real, precision=HIGHEST
    )
    reverted_real, reverted_imag = complex_times(back_real, back_imag, twist_cos, twist_sin)
    result = jnp.einsum("ka,kbc->abc", outer_cos, reverted_real, precision=HIGHEST) - jnp.einsum(
        "ka,kbc->abc", outer_sin, reverted_imag, precision=HIGHEST
    )
    return (result / total).reshape(count, whole.shape[2])


def local(
    branches,
    residual,
    segments,
    long_filter,
    short_taps,
    skip_gain,
    out_weight,
    norm_gain,
    head_weight,
):
    rows = branches.shape[0]
    channels = branches.shape[2]
    shards = lax.axis_size("seq")
    rank = lax.axis_index("seq")
    first = rank * rows
    prior = passed_along(branches[rows - 2 :], "seq", 1)
    padded = jnp.concatenate([prior, branches], axis=0).astype(jnp.float32)
    flagged_positions = jnp.concatenate([jnp.full((2,), -1, jnp.int32), segments])
    window = lax.dynamic_slice_in_dim(flagged_positions, first, rows + 2)
    own_ids = window[2:]
    featured = jnp.zeros((rows, 3, channels), jnp.float32)
    for offset in range(3):
        earlier = padded[2 - offset : 2 - offset + rows]
        same = window[2 - offset : 2 - offset + rows] == own_ids
        featured = featured + jnp.where(
            same[:, None, None], short_taps[:, offset, :][None] * earlier, 0.0
        )
    mixed = featured[:, 1] * featured[:, 2]
    signals = jnp.stack([mixed, long_filter])
    whole = lax.all_to_all(signals, "seq", split_axis=2, concat_axis=1, tiled=True)
    columns = window_convolve(whole, shards)
    conv = lax.all_to_all(columns, "seq", split_axis=0, concat_axis=1, tiled=True)
    gated = (featured[:, 0] * (conv + skip_gain * mixed)).astype(jnp.bfloat16)
    weight_rows = out_weight
    mixed_out = jnp.dot(
        lax.all_gather(gated, "tp", axis=1, tiled=True),
        weight_rows,
        preferred_element_type=jnp.float32,
    )
    hidden = (residual.astype(jnp.float32) + mixed_out).astype(jnp.bfloat16)
    width = head_weight.shape[0]
    flat_weight = head_weight.reshape(width, -1)
    local_wide = hidden.astype(jnp.float32)
    squares = jnp.sum(local_wide * local_wide, axis=1)
    total_squares = lax.psum(squares, "tp")
    scale = lax.rsqrt(total_squares / width + EPSILON)
    local_width = hidden.shape[1]
    local_gain = lax.dynamic_slice_in_dim(
        norm_gain, lax.axis_index("tp") * local_width, local_width
    )
    normed = (local_wide * scale[:, None] * local_gain).astype(jnp.bfloat16)
    weight_rows = flat_weight
    projected = jnp.dot(
        lax.all_gather(normed, "tp", axis=1, tiled=True),
        weight_rows,
        preferred_element_type=jnp.float32,
    )
    projected = projected.astype(jnp.bfloat16).reshape(rows, 3, -1, DH)
    query = projected[:, 0]
    keys = projected[:, 1]
    values = projected[:, 2]
    local_heads = query.shape[1]
    factor = 1.0 / math.sqrt(DH)
    query_pos = first + jnp.arange(rows, dtype=jnp.int32)
    peak = jnp.full((rows, local_heads), -1e30, jnp.float32)
    piece_keys = lax.all_gather(keys, "seq", axis=0, tiled=True)
    piece_values = lax.all_gather(values, "seq", axis=0, tiled=True)
    count = piece_keys.shape[0]
    score = (
        jnp.einsum("qhd,khd->qhk", query, piece_keys, preferred_element_type=jnp.float32) * factor
    )
    key_pos = jnp.arange(count, dtype=jnp.int32)
    allowed = (key_pos[None, :] <= query_pos[:, None]) & (segments[None, :] == own_ids[:, None])
    allowed = allowed[:, None, :]
    masked_scores = jnp.where(allowed, score, -1e30)
    new_peak = jnp.maximum(peak, jnp.max(masked_scores, axis=2))
    weight = jnp.where(allowed, jnp.exp(score - new_peak[:, :, None]), 0.0)
    mass = jnp.sum(weight, axis=2)
    accum = jnp.einsum(
        "qhk,khd->qhd",
        weight.astype(jnp.bfloat16),
        piece_values,
        preferred_element_type=jnp.float32,
    )
    peak, mass, accum = (new_peak, mass, accum)
    context = (accum / mass[:, :, None]).reshape(rows, local_heads * DH).astype(jnp.bfloat16)
    return (hidden, context)


def solution(mesh):
    placed = (
        P(("groups", "seq"), None, "tp"),
        P(("groups", "seq"), "tp"),
        P("groups"),
        P("seq", "tp"),
        P(None, None, "tp"),
        P("tp"),
        P(None, "tp"),
        P(),
        P(None, None, "tp"),
    )
    return jax.shard_map(
        local,
        mesh=mesh,
        in_specs=placed,
        out_specs=(P(("groups", "seq"), "tp"), P(("groups", "seq"), "tp")),
        check_vma=False,
    )
```

profile of v0, /device:TPU:0, one launch (start us, length us, event | category | flops | bytes accessed | tf_op | source)
XLA Modules:
  0.0 157.5 jit_solution(12223099710798649422)
XLA Ops:
  8.2 5.0 %collective-permute-start = (bf16[2,3,512]{0,2,1:T(8,128)(2,1)S(1)}, bf16[2,3,512]{0,2,1:T(8,128)(2,1)S(1)}, u32[]{:S(2)}, u32[]{:S(2)}) collective-permute-start(bf16[2,3,512]{0,2,1:T(8,128)(2,1)S(1)} %copy.58), channel_id=1, source_target_pairs={{0,4},{4,8},{8,12},{1,5},{5,9},{9,13},{2,6},{6,10},{10,14},{3,7},{... | collective-permute-start | bytes 18440 | tf_op jit(solution)/shard_map/ppermute | solution.py:19
  13.2 0.9 fusion.134
  14.0 0.8 pad_dynamic-slice_fusion
  14.9 1.2 copy.59
  16.1 1.1 copy.60
  17.2 4.3 %collective-permute-done = bf16[2,3,512]{0,2,1:T(8,128)(2,1)S(1)} collective-permute-done((bf16[2,3,512]{0,2,1:T(8,128)(2,1)S(1)}, bf16[2,3,512]{0,2,1:T(8,128)(2,1)S(1)}, u32[]{:S(2)}, u32[]{:S(2)}) %collective-permute-start) | collective-permute-done | bytes 6176 | tf_op jit(solution)/shard_map/ppermute | solution.py:19
  21.8 1.2 fusion.11
  23.0 1.3 pad_maximum_fusion
  24.3 5.8 %all-to-all-start = ((f32[2,128,512]{1,0,2:T(2,128)}), f32[2,128,512]{1,0,2:T(2,128)S(1)}, u32[]{:S(2)}, u32[]{:S(2)}) async-start(f32[2,128,512]{1,0,2:T(2,128)} %pad_maximum_fusion), calls=%async_computation | async-start | bytes 1048576 | tf_op jit(solution)/shard_map/all_to_all | solution.py:102
  30.5 13.2 %all-to-all-done = f32[2,128,512]{1,0,2:T(2,128)S(1)} async-done(((f32[2,128,512]{1,0,2:T(2,128)}), f32[2,128,512]{1,0,2:T(2,128)S(1)}, u32[]{:S(2)}, u32[]{:S(2)}) %all-to-all-start) | async-done | bytes 524320 | tf_op jit(solution)/shard_map/all_to_all | solution.py:102
  43.9 1.1 convolution_bitcast_fusion
  45.0 2.4 %multiply_subtract_fusion = (f32[2,8,128,128]{3,1,2,0:T(8,128)S(1)}, f32[2,8,128,128]{3,1,2,0:T(8,128)}) fusion(f32[2,8,128,128]{3,1,2,0:T(8,128)S(1)} %convolution_bitcast_fusion, f32[8,128]{0,1:T(8,128)S(1)} %copy.63, f32[8,128]{0,1:T(8,128)S(1)} %copy.62, f32[2,128,4,128]{3,2,1,0:T(4,128)S(1)} %copy.83), kind=kOutput, calls=%fused_computation.22 | convolution fusion | flops 14418368 | bytes 3678208 | tf_op jit(solution)/shard_map/ka,sabc->skbc/dot_general | solution.py:42
  47.8 2.2 %fusion.46 = f32[2,8,128,128]{3,2,1,0:T(8,128)} fusion(f32[2,8,128,128]{2,3,1,0:T(8,128)S(1)} %copy.64), kind=kOutput, calls=%fused_computation.79 | convolution fusion | flops 402882560 | bytes 2097152 | tf_op jit(solution)/shard_map/bq,skbc->skqc/dot_general | solution.py:52
  50.0 1.6 copy.65
  51.6 1.2 fusion.44
  52.8 2.4 %fusion.2 = f32[2,8,128,128]{2,3,1,0:T(8,128)S(1)} fusion(f32[2,8,128,128]{3,2,1,0:T(8,128)} %fusion.46, f32[2,8,128,128]{2,3,1,0:T(8,128)S(1)} %copy.65), kind=kOutput, calls=%fused_computation.6 | convolution fusion | flops 403144704 | bytes 3145728 | tf_op jit(solution)/shard_map/bq,skbc->skqc/dot_general | solution.py:52
  55.3 1.2 fusion.1
  56.6 0.8 fusion.20
  57.5 0.8 fusion.24
  58.3 0.8 convolution_add_fusion.2
  59.1 1.0 add_bitcast_fusion
  62.6 3.4 %all-to-all-start.1 = ((f32[4,128,128]{2,1,0:T(8,128)}), f32[4,128,128]{2,1,0:T(8,128)S(1)}, u32[]{:S(2)}, u32[]{:S(2)}) async-start(f32[4,128,128]{2,1,0:T(8,128)} %copy.70), calls=%async_computation.1 | async-start | bytes 524288 | tf_op jit(solution)/shard_map/all_to_all | solution.py:104
  66.1 8.3 %all-to-all-done.1 = f32[4,128,128]{2,1,0:T(8,128)S(1)} async-done(((f32[4,128,128]{2,1,0:T(8,128)}), f32[4,128,128]{2,1,0:T(8,128)S(1)}, u32[]{:S(2)}, u32[]{:S(2)}) %all-to-all-start.1) | async-done | bytes 262176 | tf_op jit(solution)/shard_map/all_to_all | solution.py:104
  74.7 7.2 %all_gather.12 = bf16[128,2048]{0,1:T(8,128)(2,1)S(1)} all-gather(bf16[128,512]{0,1:T(8,128)(2,1)S(1)} %fusion.32), channel_id=1, replica_groups=mesh['groups'=2,'seq'=4,'tp'=4] {'tp'}, dimensions={1}, use_global_device_ids=true | all-gather | bytes 655360 | tf_op jit(solution)/shard_map/all_gather | solution.py:108
  81.8 3.0 %fusion.14 = (f32[128]{0:T(128)S(1)}, bf16[128,1024]{1,0:T(8,128)(2,1)S(1)}) fusion(bf16[128,2048]{0,1:T(8,128)(2,1)S(1)} %all_gather.12, bf16[2048,1024]{1,0:T(8,128)(2,1)} %param.15, bf16[128,1024]{1,0:T(8,128)(2,1)S(1)} %copy-done.1), kind=kOutput, calls=%fused_computation.35 | convolution fusion | flops 537657216 | bytes 5243392 | tf_op jit(solution)/shard_map/dot_general | solution.py:107
  84.9 6.4 %psum.7 = f32[128]{0:T(128)S(1)} all-reduce(f32[128]{0:T(128)S(1)} %get-tuple-element.24), channel_id=1, replica_groups=mesh['groups'=2,'seq'=4,'tp'=4] {'tp'}, use_global_device_ids=true, to_apply=%region_1.2 | all-reduce | flops 128 | bytes 1024 | tf_op jit(solution)/shard_map/psum | solution.py:117
  91.3 0.8 fusion.16
  92.3 17.0 %copy.72 = bf16[4096,3,512]{0,2,1:T(8,128)(2,1)} copy(bf16[4096,3,512]{2,0,1:T(8,128)(2,1)} %param.17) | data formatting | bytes 25165824 | tf_op args[8]
  109.4 9.2 %convolution_convert_fusion = bf16[128,1536]{1,0:T(8,128)(2,1)S(1)} fusion(bf16[128,4096]{1,0:T(8,128)(2,1)} %all-gather.4.cloned.1.call-done, bf16[4096,1536]{0,1:T(8,128)(2,1)} %bitcast.133), kind=kOutput, calls=%fused_computation | convolution fusion | flops 1610809344 | bytes 14024704 | tf_op jit(solution)/shard_map/dot_general | solution.py:125
  118.9 15.0 %all-gather.1 = bf16[512,1,4,128]{3,0,2,1:T(8,128)(2,1)S(1)} all-gather(bf16[128,1,4,128]{3,0,2,1:T(8,128)(2,1)S(1)} %copy.88), channel_id=3, replica_groups=mesh['groups'=2,'seq'=4,'tp'=4] {'seq'}, dimensions={0}, use_global_device_ids=true | all-gather | bytes 655360 | tf_op jit(solution)/shard_map/all_gather | solution.py:138
  134.4 15.0 %all-gather = bf16[512,1,4,128]{0,3,2,1:T(8,128)(2,1)S(1)} all-gather(bf16[128,1,4,128]{0,3,2,1:T(8,128)(2,1)S(1)} %copy.87), channel_id=2, replica_groups=mesh['groups'=2,'seq'=4,'tp'=4] {'seq'}, dimensions={0}, use_global_device_ids=true | all-gather | bytes 655360 | tf_op jit(solution)/shard_map/all_gather | solution.py:139
  149.9 0.8 copy.77
  (47 shorter events, 6.8 us)
Async XLA Ops:
  8.2 13.3 %collective-permute-start = (bf16[2,3,512]{0,2,1:T(8,128)(2,1)S(1)}, bf16[2,3,512]{0,2,1:T(8,128)(2,1)S(1)}, u32[]{:S(2)}, u32[]{:S(2)}) collective-permute-start(bf16[2,3,512]{0,2,1:T(8,128)(2,1)S(1)} %copy.58), channel_id=1, source_target_pairs={{0,4},{4,8},{8,12},{1,5},{5,9},{9,13},{2,6},{6,10},{10,14},{3,7},{... | collective-permute-start | bytes 18440 | tf_op jit(solution)/shard_map/ppermute | solution.py:19
  24.3 19.4 %all-to-all-start = ((f32[2,128,512]{1,0,2:T(2,128)}), f32[2,128,512]{1,0,2:T(2,128)S(1)}, u32[]{:S(2)}, u32[]{:S(2)}) async-start(f32[2,128,512]{1,0,2:T(2,128)} %pad_maximum_fusion), calls=%async_computation | async-start | bytes 1048576 | tf_op jit(solution)/shard_map/all_to_all | solution.py:102
  59.1 15.4 %copy-start.3 = (f32[512]{0:T(512)S(1)}, f32[512]{0:T(512)}, u32[]{:S(2)}) copy-start(f32[512]{0:T(512)} %param.14) | copy-start | bytes 6148
  60.2 21.7 %copy-start.1 = (bf16[128,1024]{1,0:T(8,128)(2,1)S(1)}, bf16[128,1024]{1,0:T(8,128)(2,1)}, u32[]{:S(2)}) copy-start(bf16[128,1024]{1,0:T(8,128)(2,1)} %param.10) | copy-start | bytes 786436
  62.6 11.8 %all-to-all-start.1 = ((f32[4,128,128]{2,1,0:T(8,128)}), f32[4,128,128]{2,1,0:T(8,128)S(1)}, u32[]{:S(2)}, u32[]{:S(2)}) async-start(f32[4,128,128]{2,1,0:T(8,128)} %copy.70), calls=%async_computation.1 | async-start | bytes 524288 | tf_op jit(solution)/shard_map/all_to_all | solution.py:104
  66.0 43.4 %all-gather.4.cloned.1.call-start = ((), (), s32[]{:S(2)}) async-start(), calls=%async_computation.2 | async-start | bytes 1310720 | tf_op jit(solution)/shard_map/all_gather | solution.py:126
  66.1 25.2 %dynamic-slice-start = ((f32[4096]{0:T(1024)}, s32[]{:T(128)}), f32[1024]{0:T(1024)S(1)}, s32[]{:S(2)}) async-start(f32[4096]{0:T(1024)} %param.16, s32[]{:T(128)} %select_n.95), calls=%async_computation.3 | async-start | bytes 8704 | tf_op jit(solution)/shard_map/dynamic_slice | solution.py:120
  84.9 24.4 %copy-start = (bf16[128,1024]{1,0:T(8,128)(2,1)}, bf16[128,1024]{1,0:T(8,128)(2,1)S(1)}, u32[]{:S(2)}) copy-start(bf16[128,1024]{1,0:T(8,128)(2,1)S(1)} %get-tuple-element.25) | copy-start | bytes 786436
  92.3 17.0 %copy-start.2 = (s32[512]{0:T(512)S(1)}, s32[512]{0:T(512)}, u32[]{:S(2)}) copy-start(s32[512]{0:T(512)} %param.11) | copy-start | bytes 6148
Sparse Core Ops, SparseCore 0:
  92.3 15.5 all-gather.3
where the time goes:
time: 159 us; the launch traced here: 157 us
  blocking collectives  43.6 us (27%)
  matrix products  28.2 us (18%)
  local copies, waits for them, and re-layouts  26.9 us (17%)
  waiting for transfers between devices  25.8 us (16%)
  between operations  14.4 us (9%)
  starting transfers between devices  14.2 us (9%)
  other arithmetic  4.5 us (3%)
    unnamed x16, local copies, waits for them, and re-layouts  20.2 us
    all_gather x1, blocking collectives, local(): piece_keys = lax.all_gather(keys, 'seq', axis=0, tiled=True)  15 us
    all_gather x1, blocking collectives, local(): piece_values = lax.all_gather(values, 'seq', axis=0, tiled=True)  15 us
    all_to_all x1, waiting for transfers between devices, local(): lax.all_to_all(signals, 'seq', split_axis=2, concat_axis=1, tiled=True)  13.2 us
    dot_general x1, matrix products, local(): jnp.dot(lax.all_gather(normed, 'tp', axis=1, tiled=True), weight_rows, pr...  9.19 us
    all_to_all x1, waiting for transfers between devices, local(): lax.all_to_all(columns, 'seq', split_axis=0, concat_axis=1, tiled=True)  8.27 us
    all_gather x1, blocking collectives, local(): lax.all_gather(gated, 'tp', axis=1, tiled=True)  7.16 us
    psum x1, blocking collectives, local(): total_squares = lax.psum(squares, 'tp')  6.44 us
  transfers between devices with their start and end apart: 4, of which 3 were waited for; matrix products, arithmetic and copies ran while one was open for 14% of the time, Pallas kernels for 0%

commit v1 on v0

--- a/solution.py
+++ b/solution.py
@@ -1,6 +1,8 @@
 import math
 
 import jax
+import ml_dtypes
+import numpy as np
 import jax.numpy as jnp
 from jax import lax
 from jax.sharding import PartitionSpec as P
@@ -159,6 +161,89 @@
     return (hidden, context)
 
 
+def turn_tables(count):
+    turns = (2 * np.arange(count)[:, None] + 1) * np.arange(count)[None, :] % (4 * count)
+    angle = np.pi * turns / (2 * count)
+    table = np.concatenate([np.cos(angle), np.sin(angle)], axis=0)
+    high = table.astype(ml_dtypes.bfloat16)
+    low = (table - high.astype(np.float64)).astype(ml_dtypes.bfloat16)
+    return high, low
+
+
+def bf_dot(left, right):
+    return jnp.dot(left, right, preferred_element_type=jnp.float32)
+
+
+def aligned(
+    branches,
+    residual,
+    segments,
+    long_filter,
+    short_taps,
+    skip_gain,
+    out_weight,
+    norm_gain,
+    head_weight,
+):
+    rows = branches.shape[0]
+    channels = branches.shape[2]
+    shards = lax.axis_size("seq")
+    rank = lax.axis_index("seq")
+    first = rank * rows
+    own = channels // shards
+    count = rows * shards
+    stacked = jnp.concatenate(
+        [jnp.swapaxes(branches, 0, 1), long_filter.astype(jnp.bfloat16)[None]], axis=0
+    )
+    whole = lax.all_to_all(stacked, "seq", split_axis=2, concat_axis=1, tiled=True)
+    slots = jnp.swapaxes(head_weight, 0, 1)
+    taps = lax.dynamic_slice_in_dim(short_taps, rank * own, own, axis=2)
+    gain = lax.dynamic_slice_in_dim(skip_gain, rank * own, own)
+    inputs = whole[:3].astype(jnp.float32)
+    featured = taps[:, 0, :][:, None, :] * inputs
+    for offset in (1, 2):
+        earlier = jnp.pad(inputs, ((0, 0), (offset, 0), (0, 0)))[:, :count]
+        before = jnp.pad(segments, (offset, 0), constant_values=-1)[:count]
+        same = (before == segments)[None, :, None]
+        featured = featured + jnp.where(same, taps[:, offset, :][:, None, :] * earlier, 0.0)
+    mixed = featured[1] * featured[2]
+    high, low = turn_tables(count)
+    both = jnp.concatenate([mixed.astype(jnp.bfloat16), whole[3]], axis=1)
+    spec = bf_dot(high, both) + bf_dot(low, both)
+    mix_cos, mix_sin = spec[:count, :own], spec[count:, :own]
+    fil_cos, fil_sin = spec[:count, own:], spec[count:, own:]
+    product = jnp.concatenate(
+        [mix_cos * fil_cos - mix_sin * fil_sin, mix_cos * fil_sin + mix_sin * fil_cos], axis=0
+    ).astype(jnp.bfloat16)
+    conv = (bf_dot(high.T, product) + bf_dot(low.T, product)) / count
+    gated = (featured[0] * (conv + gain * mixed)).astype(jnp.bfloat16)
+    gated = lax.all_to_all(gated, "seq", split_axis=0, concat_axis=1, tiled=True)
+    mixed_out = bf_dot(lax.all_gather(gated, "tp", axis=1, tiled=True), out_weight)
+    hidden = (residual.astype(jnp.float32) + mixed_out).astype(jnp.bfloat16)
+    wide = lax.all_gather(hidden, "tp", axis=1, tiled=True).astype(jnp.float32)
+    scale = lax.rsqrt(jnp.mean(wide * wide, axis=1, keepdims=True) + EPSILON)
+    normed = (wide * scale * norm_gain).astype(jnp.bfloat16)
+    query, keys, values = [bf_dot(normed, slots[j]).astype(jnp.bfloat16) for j in range(3)]
+    pairs = lax.all_gather(jnp.concatenate([keys, values], axis=1), "seq", axis=0, tiled=True)
+    keys, values = pairs[:, :channels], pairs[:, channels:]
+    own_ids = lax.dynamic_slice_in_dim(segments, first, rows)
+    query_pos = first + jnp.arange(rows, dtype=jnp.int32)
+    key_pos = jnp.arange(count, dtype=jnp.int32)
+    allowed = (key_pos[None, :] <= query_pos[:, None]) & (segments[None, :] == own_ids[:, None])
+    parts = []
+    for head in range(channels // DH):
+        cols = slice(head * DH, (head + 1) * DH)
+        score = jnp.einsum(
+            "qd,kd->qk", query[:, cols], keys[:, cols], preferred_element_type=jnp.float32
+        ) / math.sqrt(DH)
+        score = jnp.where(allowed, score, -1e30)
+        weight = jnp.where(allowed, jnp.exp(score - jnp.max(score, axis=1, keepdims=True)), 0.0)
+        mass = jnp.sum(weight, axis=1, keepdims=True)
+        parts.append(bf_dot(weight.astype(jnp.bfloat16), values[:, cols]) / mass)
+    context = jnp.concatenate(parts, axis=1).astype(jnp.bfloat16)
+    return (hidden, context)
+
+
 def solution(mesh):
     placed = (
         P(("groups", "seq"), None, "tp"),
@@ -171,8 +256,14 @@
         P(),
         P(None, None, "tp"),
     )
+    def chosen(*arrays):
+        channels, rows = arrays[0].shape[2], arrays[0].shape[0]
+        shards = lax.axis_size("seq")
+        fits = channels % (shards * 128) == 0 and rows % 128 == 0 and shards * rows <= 1024
+        return aligned(*arrays) if fits else local(*arrays)
+
     return jax.shard_map(
-        local,
+        chosen,
         mesh=mesh,
         in_specs=placed,
         out_specs=(P(("groups", "seq"), "tp"), P(("groups", "seq"), "tp")),

time: 159 us -> 125 us (0.79)
  blocking collectives: 43.6 us -> 15.6 us
  waiting for transfers between devices: 25.8 us -> 52.3 us
  local copies, waits for them, and re-layouts: 26.9 us -> 4.84 us
  starting transfers between devices: 14.2 us -> 6.36 us
  matrix products: 28.2 us -> 23.8 us
  other arithmetic: 4.5 us -> 6.79 us
    all_gather x1 -> x2, waiting for transfers between devices: 0.02 us -> 40.3 us  [the longest x1 25 us: aligned(): lax.all_gather(jnp.concatenate([keys, values], axis=1), 'seq', axis=0, ti...]
    all_gather x3 -> x1, blocking collectives: 37.1 us -> 7.16 us  [aligned(): lax.all_gather(gated, 'tp', axis=1, tiled=True)]
    unnamed x16 -> x25, local copies, waits for them, and re-layouts: 20.2 us -> 2.17 us
    all_to_all x2 -> x1, waiting for transfers between devices: 21.5 us -> 12 us  [aligned(): lax.all_to_all(stacked, 'seq', split_axis=2, concat_axis=1, tiled=True)]
    all_to_all x0 -> x1, blocking collectives: none -> 8.45 us  [aligned(): lax.all_to_all(gated, 'seq', split_axis=0, concat_axis=1, tiled=True)]
    psum x1 -> x0, blocking collectives: 6.44 us -> none  [local(): total_squares = lax.psum(squares, 'tp')]
    ppermute x1 -> x0, starting transfers between devices: 4.95 us -> none  [passed_along(): return lax.ppermute(array, axis, pairs)]
    dot_general x16 -> x18, matrix products: 28.2 us -> 23.8 us  [the longest x14 19 us: bf_dot(): return jnp.dot(left, right, preferred_element_type=jnp.float32)]
  transfers between devices with their start and end apart: 4 -> 3, of which waited for: 3 -> 3; matrix products, arithmetic and copies ran while one was open for 14% -> 4% of each run, Pallas kernels for 0% -> 0%
where the time goes in v1:
time: 125 us; the launch traced here: 124 us
  waiting for transfers between devices  52.3 us (42%)
  matrix products  23.8 us (19%)
  blocking collectives  15.6 us (12%)
  between operations  14.4 us (12%)
  other arithmetic  6.79 us (5%)
  starting transfers between devices  6.36 us (5%)
  local copies, waits for them, and re-layouts  4.84 us (4%)
    all_gather x1, waiting for transfers between devices, aligned(): lax.all_gather(jnp.concatenate([keys, values], axis=1), 'seq', axis=0, ti...  25 us
    dot_general x14, matrix products, bf_dot(): return jnp.dot(left, right, preferred_element_type=jnp.float32)  19 us
    all_gather x1, waiting for transfers between devices, aligned(): wide = lax.all_gather(hidden, 'tp', axis=1, tiled=True).astype(jnp.float32)  15.3 us
    all_to_all x1, waiting for transfers between devices, aligned(): lax.all_to_all(stacked, 'seq', split_axis=2, concat_axis=1, tiled=True)  12 us
    all_to_all x1, blocking collectives, aligned(): lax.all_to_all(gated, 'seq', split_axis=0, concat_axis=1, tiled=True)  8.45 us
    all_gather x1, blocking collectives, aligned(): lax.all_gather(gated, 'tp', axis=1, tiled=True)  7.16 us
    all_to_all x1, starting transfers between devices, aligned(): lax.all_to_all(stacked, 'seq', split_axis=2, concat_axis=1, tiled=True)  6.32 us
    dot_general x4, matrix products, aligned(): jnp.einsum('qd,kd->qk', query[:, cols], keys[:, cols], preferred_element_...  4.76 us
  transfers between devices with their start and end apart: 3, of which 3 were waited for; matrix products, arithmetic and copies ran while one was open for 4% of the time, Pallas kernels for 0%

profile of v1, /device:TPU:0, one launch (start us, length us, event | category | flops | bytes accessed | tf_op | source)
XLA Modules:
  0.0 124.0 jit_solution(12234819383662647954)
XLA Ops:
  7.2 1.0 convert_bitcast_fusion
  8.3 1.3 %copy.25 = bf16[128,3,512]{0,1,2:T(4,128)(2,1)S(1)} copy(bf16[128,3,512]{2,0,1:T(8,128)(2,1)} %param.13) | data formatting | bytes 786432 | tf_op args[0]
  9.6 1.3 %pad_maximum_fusion = bf16[4,128,512]{1,0,2:T(4,128)(2,1)} fusion(bf16[1,128,512]{1,0,2:T(2,128)(2,1)S(1)} %copy.26, bf16[3,128,512]{1,0,2:T(4,128)(2,1)S(1)} %bitcast.81), kind=kLoop, calls=%fused_computation.51 | loop fusion | flops 1048576 | bytes 1048576 | tf_op jit(solution)/shard_map/concatenate | solution.py:195
  11.0 6.3 %all-to-all-start = ((bf16[4,128,512]{1,0,2:T(4,128)(2,1)}), bf16[4,128,512]{1,0,2:T(4,128)(2,1)S(1)}, u32[]{:S(2)}, u32[]{:S(2)}) async-start(bf16[4,128,512]{1,0,2:T(4,128)(2,1)} %pad_maximum_fusion), calls=%async_computation | async-start | bytes 1048576 | tf_op jit(solution)/shard_map/all_to_all | solution.py:198
  17.3 0.8 dynamic_slice.10
  18.0 0.9 constant_dynamic-slice_fusion.1
  18.9 0.9 fusion.68
  19.8 12.0 %all-to-all-done = bf16[4,128,512]{1,0,2:T(4,128)(2,1)S(1)} async-done(((bf16[4,128,512]{1,0,2:T(4,128)(2,1)}), bf16[4,128,512]{1,0,2:T(4,128)(2,1)S(1)}, u32[]{:S(2)}, u32[]{:S(2)}) %all-to-all-start) | async-done | bytes 524320 | tf_op jit(solution)/shard_map/all_to_all | solution.py:198
  31.8 0.4 copy.41
  32.7 0.7 fusion.29
  33.4 1.8 %fusion.42 = f32[256,1024]{1,0:T(8,128)S(1)} fusion(bf16[1024,512]{1,0:T(8,128)(2,1)} %constant.42.clone, bf16[512,128]{0,1:T(8,128)(2,1)S(1)} %bitcast.85, bf16[512,128]{0,1:T(8,128)(2,1)S(1)} %fusion.63), kind=kOutput, calls=%fused_computation.75 | convolution fusion | flops 268959744 | bytes 2359296 | tf_op jit(solution)/shard_map/dot_general | solution.py:174
  35.2 0.5 fusion.6
  37.2 8.4 %all_to_all.34 = bf16[4,128,128]{1,2,0:T(8,128)(2,1)S(1)} all-to-all(bf16[4,128,128]{1,2,0:T(8,128)(2,1)S(1)} %bitcast.89), channel_id=1, replica_groups=mesh['groups'=2,'seq'=4,'tp'=4] {'seq'}, dimensions={0} | all-to-all | bytes 262144 | tf_op jit(solution)/shard_map/all_to_all | solution.py:220
  45.7 7.2 %all_gather.9 = bf16[128,2048]{0,1:T(8,128)(2,1)S(1)} all-gather(bf16[128,512]{0,1:T(8,128)(2,1)S(1)} %bitcast.87), channel_id=1, replica_groups=mesh['groups'=2,'seq'=4,'tp'=4] {'tp'}, dimensions={1}, use_global_device_ids=true | all-gather | bytes 655360 | tf_op jit(solution)/shard_map/all_gather | solution.py:221
  52.8 1.5 %fusion.7 = bf16[128,1024]{1,0:T(8,128)(2,1)} fusion(bf16[128,2048]{0,1:T(8,128)(2,1)S(1)} %all_gather.9, bf16[2048,1024]{1,0:T(8,128)(2,1)S(1)} %copy-done, bf16[128,1024]{1,0:T(8,128)(2,1)S(1)} %copy-done.7), kind=kOutput, calls=%fused_computation.14 | convolution fusion | flops 537264128 | bytes 5242880 | tf_op jit(solution)/shard_map/dot_general | solution.py:174
  54.4 15.3 %all-gather.3.cloned.1.call-done = bf16[128,4096]{1,0:T(8,128)(2,1)} async-done(((bf16[128,1024]{1,0:T(8,128)(2,1)}), bf16[128,4096]{1,0:T(8,128)(2,1)}) %all-gather.3.cloned.1.call-update) | async-done | bytes 1048592 | tf_op jit(solution)/shard_map/all_gather | solution.py:223
  69.6 1.6 %fusion.3 = f32[128]{0:T(128)S(1)} fusion(bf16[128,4096]{1,0:T(8,128)(2,1)} %all-gather.3.cloned.1.call-done), kind=kLoop, calls=%fused_computation.8 | loop fusion | flops 1572736 | bytes 1049088 | tf_op jit(solution)/shard_map/reduce_sum | solution.py:224
  71.2 3.3 %fusion.18 = bf16[128,512]{1,0:T(8,128)(2,1)S(1)} fusion(bf16[3,4096,512]{2,1,0:T(8,128)(2,1)} %bitcast.91, bf16[128,4096]{1,0:T(8,128)(2,1)} %all-gather.3.cloned.1.call-done, f32[4096]{0:T(1024)S(1)} %copy-done.9, f32[128]{0:T(128)S(1)} %add_rsqrt_fusion), kind=kOutput, calls=%fused_computation.31 | convolution fusion | flops 539033600 | bytes 5390848 | tf_op jit(solution)/shard_map/dot_general | solution.py:174
  74.5 3.0 %fusion.19 = bf16[128,512]{1,0:T(8,128)(2,1)S(1)} fusion(bf16[3,4096,512]{2,1,0:T(8,128)(2,1)} %bitcast.92, bf16[128,4096]{1,0:T(8,128)(2,1)S(1)} %copy-done.2, f32[4096]{0:T(1024)S(1)} %copy-done.9, f32[128]{0:T(128)S(1)} %add_rsqrt_fusion), kind=kOutput, calls=%fused_computation.32 | convolution fusion | flops 539033600 | bytes 5390848 | tf_op jit(solution)/shard_map/dot_general | solution.py:174
  77.5 0.7 pad_maximum_fusion.2
  78.4 3.0 %fusion.17 = bf16[128,512]{1,0:T(8,128)(2,1)S(1)} fusion(bf16[3,4096,512]{2,1,0:T(8,128)(2,1)} %bitcast.93, bf16[128,4096]{1,0:T(8,128)(2,1)S(1)} %copy-done.2, f32[4096]{0:T(1024)S(1)} %copy-done.9, f32[128]{0:T(128)S(1)} %add_rsqrt_fusion), kind=kOutput, calls=%fused_computation.30 | convolution fusion | flops 539033600 | bytes 5390848 | tf_op jit(solution)/shard_map/dot_general | solution.py:174
  81.4 25.0 %all-gather.5.cloned.1.call-done = bf16[512,1024]{1,0:T(8,128)(2,1)} async-done(((bf16[128,1024]{1,0:T(8,128)(2,1)}), bf16[512,1024]{1,0:T(8,128)(2,1)}) %all-gather.5.cloned.1.call-update) | async-done | bytes 1048592 | tf_op jit(solution)/shard_map/all_gather | solution.py:227
  106.4 1.2 fusion.83
  107.6 1.2 fusion.86
  108.8 1.2 fusion.85
  110.0 1.2 fusion.84
  111.2 0.4 fusion.34
  111.6 1.2 fusion.25
  112.8 1.2 fusion.24
  114.0 1.2 fusion.23
  115.2 1.2 fusion.22
  116.4 0.8 copy.29
  (42 shorter events, 2.3 us)
Async XLA Ops:
  11.0 20.8 %all-to-all-start = ((bf16[4,128,512]{1,0,2:T(4,128)(2,1)}), bf16[4,128,512]{1,0,2:T(4,128)(2,1)S(1)}, u32[]{:S(2)}, u32[]{:S(2)}) async-start(bf16[4,128,512]{1,0,2:T(4,128)(2,1)} %pad_maximum_fusion), calls=%async_computation | async-start | bytes 1048576 | tf_op jit(solution)/shard_map/all_to_all | solution.py:198
  17.3 52.3 %all-gather.3.cloned.1.call-start = ((), (), s32[]{:S(2)}) async-start(), calls=%async_computation.2 | async-start | bytes 1310720 | tf_op jit(solution)/shard_map/all_gather | solution.py:223
  32.2 3.0 %copy-start.1 = (bf16[1024,512]{1,0:T(8,128)(2,1)S(1)}, bf16[1024,512]{1,0:T(8,128)(2,1)}, u32[]{:S(2)}) copy-start(bf16[1024,512]{1,0:T(8,128)(2,1)} %constant.43.clone) | copy-start | bytes 3145732
  33.3 2.5 %copy-start.4 = (bf16[512,512]{1,0:T(8,128)(2,1)S(1)}, bf16[512,512]{1,0:T(8,128)(2,1)}, u32[]{:S(2)}) copy-start(bf16[512,512]{1,0:T(8,128)(2,1)} %constant.54) | copy-start | bytes 1572868
  33.3 2.9 %copy-start.3 = (bf16[512,512]{1,0:T(8,128)(2,1)S(1)}, bf16[512,512]{1,0:T(8,128)(2,1)}, u32[]{:S(2)}) copy-start(bf16[512,512]{1,0:T(8,128)(2,1)} %constant.56) | copy-start | bytes 1572868
  33.4 3.1 %copy-start.6 = (bf16[512,512]{1,0:T(8,128)(2,1)S(1)}, bf16[512,512]{1,0:T(8,128)(2,1)}, u32[]{:S(2)}) copy-start(bf16[512,512]{1,0:T(8,128)(2,1)} %constant.57) | copy-start | bytes 1572868
  35.2 1.6 %copy-start.5 = (bf16[512,512]{1,0:T(8,128)(2,1)S(1)}, bf16[512,512]{1,0:T(8,128)(2,1)}, u32[]{:S(2)}) copy-start(bf16[512,512]{1,0:T(8,128)(2,1)} %constant.55) | copy-start | bytes 1572868
  35.7 17.1 %copy-start = (bf16[2048,1024]{1,0:T(8,128)(2,1)S(1)}, bf16[2048,1024]{1,0:T(8,128)(2,1)}, u32[]{:S(2)}) copy-start(bf16[2048,1024]{1,0:T(8,128)(2,1)} %param.19) | copy-start | bytes 12582916
  35.7 17.1 %copy-start.7 = (bf16[128,1024]{1,0:T(8,128)(2,1)S(1)}, bf16[128,1024]{1,0:T(8,128)(2,1)}, u32[]{:S(2)}) copy-start(bf16[128,1024]{1,0:T(8,128)(2,1)} %param.14) | copy-start | bytes 786436
  37.2 34.1 %copy-start.9 = (f32[4096]{0:T(1024)S(1)}, f32[4096]{0:T(1024)}, u32[]{:S(2)}) copy-start(f32[4096]{0:T(1024)} %param.20) | copy-start | bytes 49156
  54.3 52.1 %all-gather.5.cloned.1.call-start = ((), (), s32[]{:S(2)}) async-start(), calls=%async_computation.3 | async-start | bytes 1310720 | tf_op jit(solution)/shard_map/all_gather | solution.py:227
  69.6 4.9 %copy-start.2 = (bf16[128,4096]{1,0:T(8,128)(2,1)S(1)}, bf16[128,4096]{1,0:T(8,128)(2,1)}, u32[]{:S(2)}) copy-start(bf16[128,4096]{1,0:T(8,128)(2,1)} %all-gather.3.cloned.1.call-done) | copy-start | bytes 3145732
  74.5 3.8 %copy-start.8 = (s32[512]{0:T(512)S(1)}, s32[512]{0:T(512)}, u32[]{:S(2)}) copy-start(s32[512]{0:T(512)} %param.15) | copy-start | bytes 6148
Sparse Core Ops, SparseCore 0:
  54.4 15.1 all-gather.2
  78.4 27.9 all-gather.4

commit v2 on v0

--- a/solution.py
+++ b/solution.py
@@ -1,8 +1,13 @@
+import functools
 import math
 
 import jax
+import ml_dtypes
+import numpy as np
 import jax.numpy as jnp
 from jax import lax
+from jax.experimental import pallas as pl
+from jax.experimental.pallas import tpu as pltpu
 from jax.sharding import PartitionSpec as P
 
 DH = 128
@@ -159,6 +164,406 @@
     return (hidden, context)
 
 
+def turn_tables(count):
+    turns = (2 * np.arange(count)[:, None] + 1) * np.arange(count)[None, :] % (4 * count)
+    angle = np.pi * turns / (2 * count)
+    table = np.concatenate([np.cos(angle), np.sin(angle)], axis=0)
+    high = table.astype(ml_dtypes.bfloat16)
+    low = (table - high.astype(np.float64)).astype(ml_dtypes.bfloat16)
+    return high, low
+
+
+def bf_dot(left, right):
+    return jnp.dot(left, right, preferred_element_type=jnp.float32)
+
+
+def span(index, size):
+    return pl.ds(pl.multiple_of(index * size, size), size)
+
+
+def remote(src, dst, send, recv, **where):
+    return pltpu.make_async_remote_copy(
+        src_ref=src,
+        dst_ref=dst,
+        send_sem=send,
+        recv_sem=recv,
+        device_id=where,
+        device_id_type=pl.DeviceIdType.MESH,
+    )
+
+
+def pair_gather(buf, x, m, wide, send, recv, consume):
+    chips = m // 2
+    sibling = x + 1 - 2 * lax.rem(x, 2)
+
+    def block(i):
+        return buf.at[:, span(i, wide)]
+
+    sent = []
+
+    def ship(i, slot, peer):
+        copy = remote(block(i), block(i), send.at[slot], recv.at[slot], tp=peer)
+        copy.start()
+        sent.append(copy)
+
+    def arrive(i, slot):
+        remote(block(i), block(i), send.at[slot], recv.at[slot], tp=sibling).wait_recv()
+
+    for c in range(1, chips):
+        ship(x, c, lax.rem(x + 2 * c, m))
+    ship(x, 0, sibling)
+    consume(x)
+    arrive(sibling, 0)
+    consume(sibling)
+    for c in range(1, chips):
+        source = lax.rem(x + m - 2 * c, m)
+        arrive(source, c)
+        ship(source, chips - 1 + c, sibling)
+        consume(source)
+    for c in range(1, chips):
+        source = lax.rem(sibling + m - 2 * c, m)
+        arrive(source, chips - 1 + c)
+        consume(source)
+    return sent
+
+
+def layer_kernel(
+    n,
+    m,
+    branches,
+    filt,
+    residual,
+    segs,
+    taps,
+    skip,
+    gain,
+    high_in,
+    low_in,
+    high_t_in,
+    low_t_in,
+    out_w_in,
+    head_in,
+    hidden_out,
+    context_out,
+    fil_stage,
+    sig,
+    fil,
+    high,
+    low,
+    high_t,
+    low_t,
+    out_w,
+    head,
+    seg_wide,
+    g_send,
+    g_all,
+    acc,
+    h_all,
+    n_all,
+    squares,
+    kv_acc,
+    kv,
+    local_sem,
+    a_send,
+    a_recv,
+    f_send,
+    f_recv,
+    b_send,
+    b_recv,
+    c_send,
+    c_recv,
+    d_send,
+    d_recv,
+    k_send,
+    k_recv,
+):
+    z = lax.axis_index("seq")
+    x = lax.axis_index("tp")
+    rows, channels = filt.shape
+    count, own = fil.shape
+    width = h_all.shape[1]
+    local_width = residual.shape[1]
+    reach = kv.shape[0] - 1
+    barrier = pltpu.get_barrier_semaphore()
+    for d in range(1, n):
+        pl.semaphore_signal(
+            barrier, inc=1, device_id={"seq": lax.rem(z + d, n)}, device_id_type=pl.DeviceIdType.MESH
+        )
+    for d in range(1, m):
+        pl.semaphore_signal(
+            barrier, inc=1, device_id={"tp": lax.rem(x + d, m)}, device_id_type=pl.DeviceIdType.MESH
+        )
+    fil_stage[...] = filt[...].astype(jnp.bfloat16)
+    pl.semaphore_wait(barrier, n + m - 2)
+    sent = []
+    for d in range(1, n):
+        peer = lax.rem(z + d, n)
+        copy = remote(
+            branches.at[:, :, span(peer, own)],
+            sig.at[:, span(z, rows), :],
+            a_send.at[d],
+            a_recv.at[d],
+            seq=peer,
+        )
+        copy.start()
+        sent.append(copy)
+        copy = remote(
+            fil_stage.at[:, span(peer, own)],
+            fil.at[span(z, rows), :],
+            f_send.at[d],
+            f_recv.at[d],
+            seq=peer,
+        )
+        copy.start()
+        sent.append(copy)
+    mine = pltpu.make_async_copy(
+        branches.at[:, :, span(z, own)], sig.at[:, span(z, rows), :], local_sem.at[0]
+    )
+    mine.start()
+    loads = []
+    for i, (src, dst) in enumerate(
+        (
+            (high_in, high),
+            (low_in, low),
+            (high_t_in, high_t),
+            (low_t_in, low_t),
+            (out_w_in, out_w),
+            (head_in.at[1], head.at[1]),
+            (head_in.at[2], head.at[2]),
+            (head_in.at[0], head.at[0]),
+        )
+    ):
+        load = pltpu.make_async_copy(src, dst, local_sem.at[1 + i])
+        load.start()
+        loads.append(load)
+    fil[span(z, rows), :] = fil_stage[:, span(z, own)]
+    for d in range(1, reach + 1):
+
+        @pl.when(z < d)
+        def _(d=d):
+            kv[d] = jnp.zeros(kv.shape[1:], kv.dtype)
+
+    ids = jnp.broadcast_to(segs[...].astype(jnp.float32), (own, count)).T
+    seg_wide[...] = ids
+    place = lax.broadcasted_iota(jnp.int32, (count, own), 0)
+    same = [
+        (pltpu.roll(ids, offset, 0) == ids) & (place >= offset) for offset in (1, 2)
+    ]
+    mine.wait()
+    for d in range(1, n):
+        peer = lax.rem(z + n - d, n)
+        remote(
+            branches.at[:, :, span(peer, own)],
+            sig.at[:, span(peer, rows), :],
+            a_send.at[d],
+            a_recv.at[d],
+            seq=peer,
+        ).wait_recv()
+        remote(
+            fil_stage.at[:, span(peer, own)],
+            fil.at[span(peer, rows), :],
+            f_send.at[d],
+            f_recv.at[d],
+            seq=peer,
+        ).wait_recv()
+    featured = []
+    for j in range(3):
+        wide = sig[j].astype(jnp.float32)
+        total = taps[j, pl.ds(0, 1), span(z, own)] * wide
+        for offset in (1, 2):
+            term = taps[j, pl.ds(offset, 1), span(z, own)] * pltpu.roll(wide, offset, 0)
+            total = total + jnp.where(same[offset - 1], term, 0.0)
+        featured.append(total)
+    mixed = featured[1] * featured[2]
+    for load in loads[:4]:
+        load.wait()
+    both = jnp.concatenate([mixed.astype(jnp.bfloat16), fil[...]], axis=1)
+    spec = bf_dot(high[...], both) + bf_dot(low[...], both)
+    mix_cos, mix_sin = spec[:count, :own], spec[count:, :own]
+    fil_cos, fil_sin = spec[:count, own:], spec[count:, own:]
+    product = jnp.concatenate(
+        [mix_cos * fil_cos - mix_sin * fil_sin, mix_cos * fil_sin + mix_sin * fil_cos], axis=0
+    ).astype(jnp.bfloat16)
+    conv = (bf_dot(high_t[...], product) + bf_dot(low_t[...], product)) * (1.0 / count)
+    gated = featured[0] * (conv + skip[:, span(z, own)] * mixed)
+    g_send[...] = gated.astype(jnp.bfloat16)
+
+    def column(shard):
+        return g_all.at[:, span(x * n + shard, own)]
+
+    for d in range(1, n):
+        peer = lax.rem(z + d, n)
+        copy = remote(
+            g_send.at[span(peer, rows), :], column(z), b_send.at[d], b_recv.at[d], seq=peer
+        )
+        copy.start()
+        sent.append(copy)
+    g_all[:, span(x * n + z, own)] = g_send[span(z, rows), :]
+    acc[...] = residual[...].astype(jnp.float32)
+    loads[4].wait()
+    for d in range(1, n):
+        peer = lax.rem(z + n - d, n)
+        remote(
+            g_send.at[span(peer, rows), :], column(peer), b_send.at[d], b_recv.at[d], seq=peer
+        ).wait_recv()
+
+    def out_part(i):
+        acc[...] += bf_dot(g_all[:, span(i, channels)], out_w[span(i, channels), :])
+
+    sent += pair_gather(g_all, x, m, channels, c_send, c_recv, out_part)
+    hidden = acc[...].astype(jnp.bfloat16)
+    hidden_out[...] = hidden
+    h_all[:, span(x, local_width)] = hidden
+    squares[...] = jnp.zeros_like(squares)
+    kv_acc[...] = jnp.zeros_like(kv_acc)
+    loads[5].wait()
+    loads[6].wait()
+
+    def head_part(i):
+        block = h_all[:, span(i, local_width)].astype(jnp.float32)
+        squares[...] += jnp.sum(block * block, axis=1, keepdims=True)
+        scaled = (block * gain[:, span(i, local_width)]).astype(jnp.bfloat16)
+        n_all[:, span(i, local_width)] = scaled
+        for j in (1, 2):
+            kv_acc[j - 1] += bf_dot(scaled, head[j, span(i, local_width), :])
+
+    sent += pair_gather(h_all, x, m, local_width, d_send, d_recv, head_part)
+    scale = lax.rsqrt(squares[:, :1] * (1.0 / width) + EPSILON)
+    for j in range(2):
+        kv[0, j] = (kv_acc[j] * scale).astype(jnp.bfloat16)
+
+    def kv_copy(d, peer):
+        return remote(kv.at[0], kv.at[d], k_send.at[d], k_recv.at[d], seq=peer)
+
+    for d in range(1, reach + 1):
+
+        @pl.when(z + d < n)
+        def _(d=d):
+            kv_copy(d, z + d).start()
+
+    loads[7].wait()
+    query = (bf_dot(n_all[...], head[0]) * scale).astype(jnp.bfloat16)
+    own_ids = seg_wide[span(z, rows), :][:, :1]
+    query_pos = z * rows + lax.broadcasted_iota(jnp.int32, (rows, rows), 0)
+    allowed = []
+    for d in range(reach + 1):
+        shard = lax.max(z - d, 0)
+        key_pos = (z - d) * rows + lax.broadcasted_iota(jnp.int32, (rows, rows), 1)
+        ids = segs[:, span(shard, rows)].astype(jnp.float32)
+        allowed.append((key_pos >= 0) & (key_pos <= query_pos) & (ids == own_ids))
+    allowed = jnp.concatenate(allowed, axis=1)
+    for d in range(1, reach + 1):
+
+        @pl.when(z >= d)
+        def _(d=d):
+            kv_copy(d, z - d).wait_recv()
+
+    for h in range(channels // DH):
+        cols = slice(h * DH, (h + 1) * DH)
+        keys = jnp.concatenate([kv[d, 0, :, cols] for d in range(reach + 1)], axis=0)
+        values = jnp.concatenate([kv[d, 1, :, cols] for d in range(reach + 1)], axis=0)
+        score = lax.dot_general(
+            query[:, cols], keys, (((1,), (1,)), ((), ())), preferred_element_type=jnp.float32
+        ) * (1.0 / math.sqrt(DH))
+        score = jnp.where(allowed, score, -1e30)
+        weight = jnp.where(allowed, jnp.exp(score - jnp.max(score, axis=1, keepdims=True)), 0.0)
+        mass = jnp.sum(weight, axis=1, keepdims=True)
+        part = bf_dot(weight.astype(jnp.bfloat16), values) / mass
+        context_out[:, cols] = part.astype(jnp.bfloat16)
+    for copy in sent:
+        copy.wait_send()
+    for d in range(1, reach + 1):
+
+        @pl.when(z + d < n)
+        def _(d=d):
+            kv_copy(d, z + d).wait_send()
+
+
+def aligned(
+    branches,
+    residual,
+    segments,
+    long_filter,
+    short_taps,
+    skip_gain,
+    out_weight,
+    norm_gain,
+    head_weight,
+):
+    rows, _, channels = branches.shape
+    local_width = residual.shape[1]
+    n = lax.axis_size("seq")
+    m = lax.axis_size("tp")
+    own = channels // n
+    count = rows * n
+    width = head_weight.shape[0]
+    reach = n // 2
+    high, low = turn_tables(count)
+    vmem = pl.BlockSpec(memory_space=pltpu.VMEM)
+    hbm = pl.BlockSpec(memory_space=pl.ANY)
+    bf16, f32 = jnp.bfloat16, jnp.float32
+    dma = pltpu.SemaphoreType.DMA
+    return pl.pallas_call(
+        functools.partial(layer_kernel, n, m),
+        out_shape=(
+            jax.ShapeDtypeStruct((rows, local_width), bf16),
+            jax.ShapeDtypeStruct((rows, channels), bf16),
+        ),
+        in_specs=[hbm] + [vmem] * 6 + [hbm] * 6,
+        out_specs=(vmem, vmem),
+        scratch_shapes=[
+            pltpu.VMEM((rows, channels), bf16),
+            pltpu.VMEM((3, count, own), bf16),
+            pltpu.VMEM((count, own), bf16),
+            pltpu.VMEM((2 * count, count), bf16),
+            pltpu.VMEM((2 * count, count), bf16),
+            pltpu.VMEM((count, 2 * count), bf16),
+            pltpu.VMEM((count, 2 * count), bf16),
+            pltpu.VMEM(out_weight.shape, bf16),
+            pltpu.VMEM((3, width, channels), bf16),
+            pltpu.VMEM((count, own), f32),
+            pltpu.VMEM((count, own), bf16),
+            pltpu.VMEM((rows, m * channels), bf16),
+            pltpu.VMEM((rows, local_width), f32),
+            pltpu.VMEM((rows, width), bf16),
+            pltpu.VMEM((rows, width), bf16),
+            pltpu.VMEM((rows, 128), f32),
+            pltpu.VMEM((2, rows, channels), f32),
+            pltpu.VMEM((reach + 1, 2, rows, channels), bf16),
+            dma((9,)),
+            dma((n,)),
+            dma((n,)),
+            dma((n,)),
+            dma((n,)),
+            dma((n,)),
+            dma((n,)),
+            dma((m,)),
+            dma((m,)),
+            dma((m,)),
+            dma((m,)),
+            dma((reach + 1,)),
+            dma((reach + 1,)),
+        ],
+        compiler_params=pltpu.CompilerParams(
+            collective_id=0, has_side_effects=True, vmem_limit_bytes=50 * 2**20
+        ),
+    )(
+        jnp.swapaxes(branches, 0, 1),
+        long_filter,
+        residual,
+        segments.reshape(1, -1),
+        short_taps,
+        skip_gain.reshape(1, -1),
+        norm_gain.reshape(1, -1),
+        high,
+        low,
+        np.ascontiguousarray(high.T),
+        np.ascontiguousarray(low.T),
+        out_weight,
+        jnp.swapaxes(head_weight, 0, 1),
+    )
+
+
 def solution(mesh):
     placed = (
         P(("groups", "seq"), None, "tp"),
@@ -171,8 +576,15 @@
         P(),
         P(None, None, "tp"),
     )
+    def chosen(*arrays):
+        channels, rows = arrays[0].shape[2], arrays[0].shape[0]
+        shards = lax.axis_size("seq")
+        fits = channels % (shards * 128) == 0 and rows % 128 == 0 and shards * rows <= 1024
+        fits = fits and shards % 2 == 0 and lax.axis_size("tp") % 2 == 0
+        return aligned(*arrays) if fits else local(*arrays)
+
     return jax.shard_map(
-        local,
+        chosen,
         mesh=mesh,
         in_specs=placed,
         out_specs=(P(("groups", "seq"), "tp"), P(("groups", "seq"), "tp")),

time: 159 us -> 67 us (0.42)
  the two profiles are of different devices: /device:TPU:0 before, /device:TPU:30 now
where the time goes in v2:
time: 67 us; the launch traced here: 66.6 us
  Pallas kernels  56.4 us (84%)
  local copies, waits for them, and re-layouts  9.51 us (14%)
    pallas_call x1, Pallas kernels, aligned(): pl.pallas_call(functools.partial(layer_kernel, n, m), out_shape=(jax.Shap...  56.4 us
    unnamed x20, local copies, waits for them, and re-layouts  9.51 us

profile of v2, /device:TPU:30, one launch (start us, length us, event | category | flops | bytes accessed | tf_op | source)
XLA Modules:
  0.0 66.6 jit_solution(8686075922795502618)
XLA Ops:
  0.6 0.0 copy-start
  0.6 1.2 %copy-done = bf16[1024,512]{1,0:T(8,128)(2,1)S(1)} copy-done((bf16[1024,512]{1,0:T(8,128)(2,1)S(1)}, bf16[1024,512]{1,0:T(8,128)(2,1)}, u32[]{:S(2)}) %copy-start) | copy-done | bytes 1048600
  1.9 0.0 copy-start.1
  1.9 1.2 %copy-done.1 = bf16[1024,512]{1,0:T(8,128)(2,1)S(1)} copy-done((bf16[1024,512]{1,0:T(8,128)(2,1)S(1)}, bf16[1024,512]{1,0:T(8,128)(2,1)}, u32[]{:S(2)}) %copy-start.1) | copy-done | bytes 1048600
  3.1 0.0 copy-start.2
  3.1 1.0 %copy-done.2 = bf16[128,3,512]{2,0,1:T(8,128)(2,1)S(1)} copy-done((bf16[128,3,512]{2,0,1:T(8,128)(2,1)S(1)}, bf16[128,3,512]{2,0,1:T(8,128)(2,1)}, u32[]{:S(2)}) %copy-start.2) | copy-done | bytes 393240
  4.1 0.0 copy-start.3
  4.1 0.9 %copy-done.3 = f32[128,512]{1,0:T(8,128)S(1)} copy-done((f32[128,512]{1,0:T(8,128)S(1)}, f32[128,512]{1,0:T(8,128)}, u32[]{:S(2)}) %copy-start.3) | copy-done | bytes 262168
  5.0 0.0 copy-start.4
  5.0 0.9 %copy-done.4 = bf16[128,1024]{1,0:T(8,128)(2,1)S(1)} copy-done((bf16[128,1024]{1,0:T(8,128)(2,1)S(1)}, bf16[128,1024]{1,0:T(8,128)(2,1)}, u32[]{:S(2)}) %copy-start.4) | copy-done | bytes 262168
  6.0 0.0 copy-start.5
  6.0 0.7 %copy-done.5 = f32[3,3,512]{2,1,0:T(4,128)S(1)} copy-done((f32[3,3,512]{2,1,0:T(4,128)S(1)}, f32[3,3,512]{2,1,0:T(4,128)}, u32[]{:S(2)}) %copy-start.5) | copy-done | bytes 18456
  6.7 0.0 copy-start.6
  6.7 0.7 %copy-done.6 = f32[4096]{0:T(1024)S(1)} copy-done((f32[4096]{0:T(1024)S(1)}, f32[4096]{0:T(1024)}, u32[]{:S(2)}) %copy-start.6) | copy-done | bytes 16408
  7.4 0.0 copy-start.7
  7.4 0.7 %copy-done.7 = s32[512]{0:T(512)S(1)} copy-done((s32[512]{0:T(512)S(1)}, s32[512]{0:T(512)}, u32[]{:S(2)}) %copy-start.7) | copy-done | bytes 2072
  8.1 0.0 copy-start.8
  8.1 0.7 %copy-done.8 = f32[512]{0:T(512)S(1)} copy-done((f32[512]{0:T(512)S(1)}, f32[512]{0:T(512)}, u32[]{:S(2)}) %copy-start.8) | copy-done | bytes 2072
  8.8 56.4 %shard_map.140 = (bf16[128,1024]{1,0:T(8,128)(2,1)S(1)}, bf16[128,512]{1,0:T(8,128)(2,1)S(1)}) custom-call(bf16[3,128,512]{2,1,0:T(8,128)(2,1)S(1)} %bitcast.5, f32[128,512]{1,0:T(8,128)S(1)} %copy-done.3, bf16[128,1024]{1,0:T(8,128)(2,1)S(1)} %copy-done.4, s32[1,512]{1,0:T(1,128)S(1)} %bitcast.7, f32[3,3,512]{2,1,0:T(4,128)S(1)} %copy-done.5, ...), custom_call_target="tpu_custom_call" | custom-call | tf_op jit(solution)/shard_map/pallas_call | solution.py:506
  65.2 0.7 %copy.17 = bf16[128,1024]{1,0:T(8,128)(2,1)} copy(bf16[128,1024]{1,0:T(8,128)(2,1)S(1)} %get-tuple-element.4) | data formatting | bytes 524288
  65.9 0.7 copy.18
Async XLA Ops:
  0.6 1.2 %copy-start = (bf16[1024,512]{1,0:T(8,128)(2,1)S(1)}, bf16[1024,512]{1,0:T(8,128)(2,1)}, u32[]{:S(2)}) copy-start(bf16[1024,512]{1,0:T(8,128)(2,1)} %constant.9.clone.low_in) | copy-start | bytes 3145732
  1.9 1.2 %copy-start.1 = (bf16[1024,512]{1,0:T(8,128)(2,1)S(1)}, bf16[1024,512]{1,0:T(8,128)(2,1)}, u32[]{:S(2)}) copy-start(bf16[1024,512]{1,0:T(8,128)(2,1)} %constant.8.clone.high_in) | copy-start | bytes 3145732
  3.1 1.0 %copy-start.2 = (bf16[128,3,512]{2,0,1:T(8,128)(2,1)S(1)}, bf16[128,3,512]{2,0,1:T(8,128)(2,1)}, u32[]{:S(2)}) copy-start(bf16[128,3,512]{2,0,1:T(8,128)(2,1)} %param.13) | copy-start | bytes 1179652
  4.1 0.9 %copy-start.3 = (f32[128,512]{1,0:T(8,128)S(1)}, f32[128,512]{1,0:T(8,128)}, u32[]{:S(2)}) copy-start(f32[128,512]{1,0:T(8,128)} %filt.1) | copy-start | bytes 786436
  5.0 0.9 %copy-start.4 = (bf16[128,1024]{1,0:T(8,128)(2,1)S(1)}, bf16[128,1024]{1,0:T(8,128)(2,1)}, u32[]{:S(2)}) copy-start(bf16[128,1024]{1,0:T(8,128)(2,1)} %residual.1) | copy-start | bytes 786436
  6.0 0.7 %copy-start.5 = (f32[3,3,512]{2,1,0:T(4,128)S(1)}, f32[3,3,512]{2,1,0:T(4,128)}, u32[]{:S(2)}) copy-start(f32[3,3,512]{2,1,0:T(4,128)} %taps.1) | copy-start | bytes 55300
  6.7 0.7 %copy-start.6 = (f32[4096]{0:T(1024)S(1)}, f32[4096]{0:T(1024)}, u32[]{:S(2)}) copy-start(f32[4096]{0:T(1024)} %param.20) | copy-start | bytes 49156
  7.4 0.7 %copy-start.7 = (s32[512]{0:T(512)S(1)}, s32[512]{0:T(512)}, u32[]{:S(2)}) copy-start(s32[512]{0:T(512)} %param.15) | copy-start | bytes 6148
  8.1 0.7 %copy-start.8 = (f32[512]{0:T(512)S(1)}, f32[512]{0:T(512)}, u32[]{:S(2)}) copy-start(f32[512]{0:T(512)} %param.18) | copy-start | bytes 6148

commit v3 on v2

--- a/solution.py
+++ b/solution.py
@@ -231,12 +231,12 @@
     n,
     m,
     branches,
-    filt,
-    residual,
-    segs,
-    taps,
-    skip,
-    gain,
+    filt_in,
+    residual_in,
+    segs_in,
+    taps_in,
+    skip_in,
+    gain_in,
     high_in,
     low_in,
     high_t_in,
@@ -245,6 +245,13 @@
     head_in,
     hidden_out,
     context_out,
+    filt,
+    residual,
+    segs,
+    taps,
+    skip,
+    gain,
+    ctx,
     fil_stage,
     sig,
     fil,
@@ -293,20 +300,41 @@
         pl.semaphore_signal(
             barrier, inc=1, device_id={"tp": lax.rem(x + d, m)}, device_id_type=pl.DeviceIdType.MESH
         )
-    fil_stage[...] = filt[...].astype(jnp.bfloat16)
+    early = []
+    for i, (src, dst) in enumerate(
+        (
+            (filt_in, filt),
+            (segs_in, segs),
+            (taps_in, taps),
+            (skip_in, skip),
+            (residual_in, residual),
+            (gain_in, gain),
+        )
+    ):
+        load = pltpu.make_async_copy(src, dst, local_sem.at[9 + i])
+        load.start()
+        early.append(load)
     pl.semaphore_wait(barrier, n + m - 2)
     sent = []
-    for d in range(1, n):
-        peer = lax.rem(z + d, n)
-        copy = remote(
-            branches.at[:, :, span(peer, own)],
-            sig.at[:, span(z, rows), :],
-            a_send.at[d],
-            a_recv.at[d],
+
+    def sig_copy(kind, d, peer, source):
+        part = pl.ds(1, 2) if kind == 0 else pl.ds(0, 1)
+        return remote(
+            branches.at[part, :, span(peer, own)],
+            sig.at[part, span(source, rows), :],
+            a_send.at[kind, d],
+            a_recv.at[kind, d],
             seq=peer,
         )
+
+    for d in range(1, n):
+        copy = sig_copy(0, d, lax.rem(z + d, n), z)
         copy.start()
         sent.append(copy)
+    early[0].wait()
+    fil_stage[...] = filt[...].astype(jnp.bfloat16)
+    for d in range(1, n):
+        peer = lax.rem(z + d, n)
         copy = remote(
             fil_stage.at[:, span(peer, own)],
             fil.at[span(z, rows), :],
@@ -314,6 +342,10 @@
             f_recv.at[d],
             seq=peer,
         )
+        copy.start()
+        sent.append(copy)
+    for d in range(1, n):
+        copy = sig_copy(1, d, lax.rem(z + d, n), z)
         copy.start()
         sent.append(copy)
     mine = pltpu.make_async_copy(
@@ -343,6 +375,7 @@
         def _(d=d):
             kv[d] = jnp.zeros(kv.shape[1:], kv.dtype)
 
+    early[1].wait()
     ids = jnp.broadcast_to(segs[...].astype(jnp.float32), (own, count)).T
     seg_wide[...] = ids
     place = lax.broadcasted_iota(jnp.int32, (count, own), 0)
@@ -352,13 +385,7 @@
     mine.wait()
     for d in range(1, n):
         peer = lax.rem(z + n - d, n)
-        remote(
-            branches.at[:, :, span(peer, own)],
-            sig.at[:, span(peer, rows), :],
-            a_send.at[d],
-            a_recv.at[d],
-            seq=peer,
-        ).wait_recv()
+        sig_copy(0, d, peer, peer).wait_recv()
         remote(
             fil_stage.at[:, span(peer, own)],
             fil.at[span(peer, rows), :],
@@ -366,15 +393,17 @@
             f_recv.at[d],
             seq=peer,
         ).wait_recv()
-    featured = []
-    for j in range(3):
+    early[2].wait()
+
+    def feature(j):
         wide = sig[j].astype(jnp.float32)
         total = taps[j, pl.ds(0, 1), span(z, own)] * wide
         for offset in (1, 2):
             term = taps[j, pl.ds(offset, 1), span(z, own)] * pltpu.roll(wide, offset, 0)
             total = total + jnp.where(same[offset - 1], term, 0.0)
-        featured.append(total)
-    mixed = featured[1] * featured[2]
+        return total
+
+    mixed = feature(1) * feature(2)
     for load in loads[:4]:
         load.wait()
     both = jnp.concatenate([mixed.astype(jnp.bfloat16), fil[...]], axis=1)
@@ -385,7 +414,11 @@
         [mix_cos * fil_cos - mix_sin * fil_sin, mix_cos * fil_sin + mix_sin * fil_cos], axis=0
     ).astype(jnp.bfloat16)
     conv = (bf_dot(high_t[...], product) + bf_dot(low_t[...], product)) * (1.0 / count)
-    gated = featured[0] * (conv + skip[:, span(z, own)] * mixed)
+    early[3].wait()
+    for d in range(1, n):
+        peer = lax.rem(z + n - d, n)
+        sig_copy(1, d, peer, peer).wait_recv()
+    gated = feature(0) * (conv + skip[:, span(z, own)] * mixed)
     g_send[...] = gated.astype(jnp.bfloat16)
 
     def column(shard):
@@ -399,6 +432,7 @@
         copy.start()
         sent.append(copy)
     g_all[:, span(x * n + z, own)] = g_send[span(z, rows), :]
+    early[4].wait()
     acc[...] = residual[...].astype(jnp.float32)
     loads[4].wait()
     for d in range(1, n):
@@ -412,8 +446,12 @@
 
     sent += pair_gather(g_all, x, m, channels, c_send, c_recv, out_part)
     hidden = acc[...].astype(jnp.bfloat16)
-    hidden_out[...] = hidden
     h_all[:, span(x, local_width)] = hidden
+    written = [
+        pltpu.make_async_copy(h_all.at[:, span(x, local_width)], hidden_out, local_sem.at[15])
+    ]
+    written[0].start()
+    early[5].wait()
     squares[...] = jnp.zeros_like(squares)
     kv_acc[...] = jnp.zeros_like(kv_acc)
     loads[5].wait()
@@ -432,14 +470,20 @@
     for j in range(2):
         kv[0, j] = (kv_acc[j] * scale).astype(jnp.bfloat16)
 
-    def kv_copy(d, peer):
-        return remote(kv.at[0], kv.at[d], k_send.at[d], k_recv.at[d], seq=peer)
-
-    for d in range(1, reach + 1):
-
-        @pl.when(z + d < n)
-        def _(d=d):
-            kv_copy(d, z + d).start()
+    def kv_copy(d, part):
+        return remote(
+            kv.at[d - 1, part],
+            kv.at[d, part],
+            k_send.at[d, part],
+            k_recv.at[d, part],
+            seq=lax.rem(z + 1, n),
+        )
+
+    for part in range(2):
+
+        @pl.when(z + 1 < n)
+        def _(part=part):
+            kv_copy(1, part).start()
 
     loads[7].wait()
     query = (bf_dot(n_all[...], head[0]) * scale).astype(jnp.bfloat16)
@@ -453,10 +497,17 @@
         allowed.append((key_pos >= 0) & (key_pos <= query_pos) & (ids == own_ids))
     allowed = jnp.concatenate(allowed, axis=1)
     for d in range(1, reach + 1):
-
-        @pl.when(z >= d)
-        def _(d=d):
-            kv_copy(d, z - d).wait_recv()
+        for part in range(2):
+
+            @pl.when(z >= d)
+            def _(d=d, part=part):
+                kv_copy(d, part).wait_recv()
+
+            if d < reach:
+
+                @pl.when(jnp.logical_and(z >= d, z + 1 < n))
+                def _(d=d, part=part):
+                    kv_copy(d + 1, part).start()
 
     for h in range(channels // DH):
         cols = slice(h * DH, (h + 1) * DH)
@@ -469,14 +520,20 @@
         weight = jnp.where(allowed, jnp.exp(score - jnp.max(score, axis=1, keepdims=True)), 0.0)
         mass = jnp.sum(weight, axis=1, keepdims=True)
         part = bf_dot(weight.astype(jnp.bfloat16), values) / mass
-        context_out[:, cols] = part.astype(jnp.bfloat16)
+        ctx[:, cols] = part.astype(jnp.bfloat16)
+    written.append(pltpu.make_async_copy(ctx, context_out, local_sem.at[0]))
+    written[1].start()
     for copy in sent:
         copy.wait_send()
     for d in range(1, reach + 1):
-
-        @pl.when(z + d < n)
-        def _(d=d):
-            kv_copy(d, z + d).wait_send()
+        for part in range(2):
+
+            @pl.when(jnp.logical_and(z >= d - 1, z + 1 < n))
+            def _(d=d, part=part):
+                kv_copy(d, part).wait_send()
+
+    for copy in written:
+        copy.wait()
 
 
 def aligned(
@@ -499,8 +556,7 @@
     width = head_weight.shape[0]
     reach = n // 2
     high, low = turn_tables(count)
-    vmem = pl.BlockSpec(memory_space=pltpu.VMEM)
-    hbm = pl.BlockSpec(memory_space=pl.ANY)
+    hbm = pl.BlockSpec(memory_space=pltpu.HBM)
     bf16, f32 = jnp.bfloat16, jnp.float32
     dma = pltpu.SemaphoreType.DMA
     return pl.pallas_call(
@@ -509,9 +565,16 @@
             jax.ShapeDtypeStruct((rows, local_width), bf16),
             jax.ShapeDtypeStruct((rows, channels), bf16),
         ),
-        in_specs=[hbm] + [vmem] * 6 + [hbm] * 6,
-        out_specs=(vmem, vmem),
+        in_specs=[hbm] * 13,
+        out_specs=(hbm, hbm),
         scratch_shapes=[
+            pltpu.VMEM((rows, channels), f32),
+            pltpu.VMEM((rows, local_width), bf16),
+            pltpu.VMEM((1, count), jnp.int32),
+            pltpu.VMEM(short_taps.shape, f32),
+            pltpu.VMEM((1, channels), f32),
+            pltpu.VMEM((1, width), f32),
+            pltpu.VMEM((rows, channels), bf16),
             pltpu.VMEM((rows, channels), bf16),
             pltpu.VMEM((3, count, own), bf16),
             pltpu.VMEM((count, own), bf16),
@@ -530,9 +593,9 @@
             pltpu.VMEM((rows, 128), f32),
             pltpu.VMEM((2, rows, channels), f32),
             pltpu.VMEM((reach + 1, 2, rows, channels), bf16),
-            dma((9,)),
-            dma((n,)),
-            dma((n,)),
+            dma((16,)),
+            dma((2, n)),
+            dma((2, n)),
             dma((n,)),
             dma((n,)),
             dma((n,)),
@@ -541,11 +604,11 @@
             dma((m,)),
             dma((m,)),
             dma((m,)),
-            dma((reach + 1,)),
-            dma((reach + 1,)),
+            dma((reach + 1, 2)),
+            dma((reach + 1, 2)),
         ],
         compiler_params=pltpu.CompilerParams(
-            collective_id=0, has_side_effects=True, vmem_limit_bytes=50 * 2**20
+            collective_id=0, has_side_effects=True, vmem_limit_bytes=62 * 2**20
         ),
     )(
         jnp.swapaxes(branches, 0, 1),

time: 67 us -> 55.3 us (0.83)
  local copies, waits for them, and re-layouts: 9.51 us -> 3.24 us
  Pallas kernels: 56.4 us -> 50.6 us
    unnamed x20 -> x2, local copies, waits for them, and re-layouts: 9.51 us -> 3.24 us
    pallas_call x1, Pallas kernels: 56.4 us -> 50.6 us  [aligned(): pl.pallas_call(functools.partial(layer_kernel, n, m), out_shape=(jax.Shap...]
where the time goes in v3:
time: 55.3 us; the launch traced here: 54.5 us
  Pallas kernels  50.6 us (92%)
  local copies, waits for them, and re-layouts  3.24 us (6%)
  between operations  0.64 us (1%)
    pallas_call x1, Pallas kernels, aligned(): pl.pallas_call(functools.partial(layer_kernel, n, m), out_shape=(jax.Shap...  50.6 us
    unnamed x2, local copies, waits for them, and re-layouts  3.24 us

profile of v3, /device:TPU:30, one launch (start us, length us, event | category | flops | bytes accessed | tf_op | source)
XLA Modules:
  0.0 54.5 jit_solution(17989901023899042309)
XLA Ops:
  0.6 50.6 %shard_map.140 = (bf16[128,1024]{1,0:T(8,128)(2,1)}, bf16[128,512]{1,0:T(8,128)(2,1)}) custom-call(bf16[3,128,512]{2,1,0:T(8,128)(2,1)} %bitcast.6, f32[128,512]{1,0:T(8,128)} %filt_in.1, bf16[128,1024]{1,0:T(8,128)(2,1)} %residual_in.1, s32[1,512]{1,0:T(1,128)} %bitcast.8, f32[3,3,512]{2,1,0:T(4,128)} %taps_in.1, f32[1,512]{1,0:T(1,128)} %bitcast.9, ...), custom_call_target="tpu_custom_call" | custom-call | tf_op jit(solution)/shard_map/pallas_call | solution.py:562
  51.2 1.7 %copy.17 = bf16[128,1024]{1,0:T(8,128)(2,1)} copy(bf16[128,1024]{1,0:T(8,128)(2,1)} %get-tuple-element.4) | data formatting | bytes 524288
  52.9 1.6 %copy.18 = bf16[128,512]{1,0:T(8,128)(2,1)} copy(bf16[128,512]{1,0:T(8,128)(2,1)} %get-tuple-element.5) | data formatting | bytes 262144

commit v4 on v3

--- a/solution.py
+++ b/solution.py
@@ -192,38 +192,47 @@
     )
 
 
-def pair_gather(buf, x, m, wide, send, recv, consume):
+def pair_gather(buf, x, m, wide, parts, send, recv, consume):
     chips = m // 2
     sibling = x + 1 - 2 * lax.rem(x, 2)
 
-    def block(i):
-        return buf.at[:, span(i, wide)]
+    def block(i, p):
+        return buf.at[:, span(i * parts + p, wide // parts)]
 
     sent = []
 
-    def ship(i, slot, peer):
-        copy = remote(block(i), block(i), send.at[slot], recv.at[slot], tp=peer)
+    def ship(i, p, slot, peer):
+        copy = remote(block(i, p), block(i, p), send.at[slot, p], recv.at[slot, p], tp=peer)
         copy.start()
         sent.append(copy)
 
-    def arrive(i, slot):
-        remote(block(i), block(i), send.at[slot], recv.at[slot], tp=sibling).wait_recv()
+    def arrive(i, p, slot):
+        remote(
+            block(i, p), block(i, p), send.at[slot, p], recv.at[slot, p], tp=sibling
+        ).wait_recv()
 
     for c in range(1, chips):
-        ship(x, c, lax.rem(x + 2 * c, m))
-    ship(x, 0, sibling)
-    consume(x)
-    arrive(sibling, 0)
-    consume(sibling)
+        for p in range(parts):
+            ship(x, p, c, lax.rem(x + 2 * c, m))
+    for p in range(parts):
+        ship(x, p, 0, sibling)
+    for p in range(parts):
+        consume(x * parts + p)
+    for p in range(parts):
+        arrive(sibling, p, 0)
+        consume(sibling * parts + p)
     for c in range(1, chips):
-        source = lax.rem(x + m - 2 * c, m)
-        arrive(source, c)
-        ship(source, chips - 1 + c, sibling)
-        consume(source)
-    for c in range(1, chips):
-        source = lax.rem(sibling + m - 2 * c, m)
-        arrive(source, chips - 1 + c)
-        consume(source)
+        near = lax.rem(x + m - 2 * c, m)
+        far = lax.rem(sibling + m - 2 * c, m)
+        for p in range(parts):
+            arrive(near, p, c)
+            ship(near, p, chips - 1 + c, sibling)
+            consume(near * parts + p)
+            if p > 0:
+                arrive(far, p - 1, chips - 1 + c)
+                consume(far * parts + p - 1)
+        arrive(far, parts - 1, chips - 1 + c)
+        consume(far * parts + parts - 1)
     return sent
 
 
@@ -441,10 +450,13 @@
             g_send.at[span(peer, rows), :], column(peer), b_send.at[d], b_recv.at[d], seq=peer
         ).wait_recv()
 
+    out_parts, head_parts = c_send.shape[1], d_send.shape[1]
+    out_step, head_step = channels // out_parts, local_width // head_parts
+
     def out_part(i):
-        acc[...] += bf_dot(g_all[:, span(i, channels)], out_w[span(i, channels), :])
-
-    sent += pair_gather(g_all, x, m, channels, c_send, c_recv, out_part)
+        acc[...] += bf_dot(g_all[:, span(i, out_step)], out_w[span(i, out_step), :])
+
+    sent += pair_gather(g_all, x, m, channels, out_parts, c_send, c_recv, out_part)
     hidden = acc[...].astype(jnp.bfloat16)
     h_all[:, span(x, local_width)] = hidden
     written = [
@@ -458,14 +470,14 @@
     loads[6].wait()
 
     def head_part(i):
-        block = h_all[:, span(i, local_width)].astype(jnp.float32)
+        block = h_all[:, span(i, head_step)].astype(jnp.float32)
         squares[...] += jnp.sum(block * block, axis=1, keepdims=True)
-        scaled = (block * gain[:, span(i, local_width)]).astype(jnp.bfloat16)
-        n_all[:, span(i, local_width)] = scaled
+        scaled = (block * gain[:, span(i, head_step)]).astype(jnp.bfloat16)
+        n_all[:, span(i, head_step)] = scaled
         for j in (1, 2):
-            kv_acc[j - 1] += bf_dot(scaled, head[j, span(i, local_width), :])
-
-    sent += pair_gather(h_all, x, m, local_width, d_send, d_recv, head_part)
+            kv_acc[j - 1] += bf_dot(scaled, head[j, span(i, head_step), :])
+
+    sent += pair_gather(h_all, x, m, local_width, head_parts, d_send, d_recv, head_part)
     scale = lax.rsqrt(squares[:, :1] * (1.0 / width) + EPSILON)
     for j in range(2):
         kv[0, j] = (kv_acc[j] * scale).astype(jnp.bfloat16)
@@ -496,31 +508,47 @@
         ids = segs[:, span(shard, rows)].astype(jnp.float32)
         allowed.append((key_pos >= 0) & (key_pos <= query_pos) & (ids == own_ids))
     allowed = jnp.concatenate(allowed, axis=1)
+    heads = [slice(h * DH, (h + 1) * DH) for h in range(channels // DH)]
+
+    def scores(d):
+        return [
+            lax.dot_general(
+                query[:, cols],
+                kv[d, 0, :, cols],
+                (((1,), (1,)), ((), ())),
+                preferred_element_type=jnp.float32,
+            )
+            for cols in heads
+        ]
+
+    def receive(d, part):
+        @pl.when(z >= d)
+        def _():
+            kv_copy(d, part).wait_recv()
+
+        if d < reach:
+
+            @pl.when(jnp.logical_and(z >= d, z + 1 < n))
+            def _():
+                kv_copy(d + 1, part).start()
+
+    found = [scores(0)]
     for d in range(1, reach + 1):
-        for part in range(2):
-
-            @pl.when(z >= d)
-            def _(d=d, part=part):
-                kv_copy(d, part).wait_recv()
-
-            if d < reach:
-
-                @pl.when(jnp.logical_and(z >= d, z + 1 < n))
-                def _(d=d, part=part):
-                    kv_copy(d + 1, part).start()
-
-    for h in range(channels // DH):
-        cols = slice(h * DH, (h + 1) * DH)
-        keys = jnp.concatenate([kv[d, 0, :, cols] for d in range(reach + 1)], axis=0)
-        values = jnp.concatenate([kv[d, 1, :, cols] for d in range(reach + 1)], axis=0)
-        score = lax.dot_general(
-            query[:, cols], keys, (((1,), (1,)), ((), ())), preferred_element_type=jnp.float32
-        ) * (1.0 / math.sqrt(DH))
-        score = jnp.where(allowed, score, -1e30)
+        receive(d, 0)
+        found.append(scores(d))
+        if d < reach:
+            receive(d, 1)
+    weights = []
+    for h in range(len(heads)):
+        score = jnp.concatenate([block[h] for block in found], axis=1)
+        score = jnp.where(allowed, score * (1.0 / math.sqrt(DH)), -1e30)
         weight = jnp.where(allowed, jnp.exp(score - jnp.max(score, axis=1, keepdims=True)), 0.0)
         mass = jnp.sum(weight, axis=1, keepdims=True)
-        part = bf_dot(weight.astype(jnp.bfloat16), values) / mass
-        ctx[:, cols] = part.astype(jnp.bfloat16)
+        weights.append((weight.astype(jnp.bfloat16), mass))
+    receive(reach, 1)
+    for (weight, mass), cols in zip(weights, heads):
+        values = jnp.concatenate([kv[d, 1, :, cols] for d in range(reach + 1)], axis=0)
+        ctx[:, cols] = (bf_dot(weight, values) / mass).astype(jnp.bfloat16)
     written.append(pltpu.make_async_copy(ctx, context_out, local_sem.at[0]))
     written[1].start()
     for copy in sent:
@@ -600,10 +628,10 @@
             dma((n,)),
             dma((n,)),
             dma((n,)),
-            dma((m,)),
-            dma((m,)),
-            dma((m,)),
-            dma((m,)),
+            dma((m, 2)),
+            dma((m, 2)),
+            dma((m, 4)),
+            dma((m, 4)),
             dma((reach + 1, 2)),
             dma((reach + 1, 2)),
         ],
@@ -642,7 +670,7 @@
     def chosen(*arrays):
         channels, rows = arrays[0].shape[2], arrays[0].shape[0]
         shards = lax.axis_size("seq")
-        fits = channels % (shards * 128) == 0 and rows % 128 == 0 and shards * rows <= 1024
+        fits = channels % (shards * 128) == 0 and arrays[1].shape[1] % 512 == 0 and rows % 128 == 0 and shards * rows <= 1024
         fits = fits and shards % 2 == 0 and lax.axis_size("tp") % 2 == 0
         return aligned(*arrays) if fits else local(*arrays)
 

time: 55.3 us -> 54.2 us (0.980)
  Pallas kernels: 50.6 us -> 49.4 us
    pallas_call x1, Pallas kernels: 50.6 us -> 49.4 us  [aligned(): pl.pallas_call(functools.partial(layer_kernel, n, m), out_shape=(jax.Shap...]
where the time goes in v4:
time: 54.2 us; the launch traced here: 53.3 us
  Pallas kernels  49.4 us (91%)
  local copies, waits for them, and re-layouts  3.24 us (6%)
  between operations  0.64 us (1%)
    pallas_call x1, Pallas kernels, aligned(): pl.pallas_call(functools.partial(layer_kernel, n, m), out_shape=(jax.Shap...  49.4 us
    unnamed x2, local copies, waits for them, and re-layouts  3.24 us

profile of v4, /device:TPU:30, one launch (start us, length us, event | category | flops | bytes accessed | tf_op | source)
XLA Modules:
  0.0 53.3 jit_solution(12332062864898915252)
XLA Ops:
  0.6 49.4 %shard_map.140 = (bf16[128,1024]{1,0:T(8,128)(2,1)}, bf16[128,512]{1,0:T(8,128)(2,1)}) custom-call(bf16[3,128,512]{2,1,0:T(8,128)(2,1)} %bitcast.6, f32[128,512]{1,0:T(8,128)} %filt_in.1, bf16[128,1024]{1,0:T(8,128)(2,1)} %residual_in.1, s32[1,512]{1,0:T(1,128)} %bitcast.8, f32[3,3,512]{2,1,0:T(4,128)} %taps_in.1, f32[1,512]{1,0:T(1,128)} %bitcast.9, ...), custom_call_target="tpu_custom_call" | custom-call | tf_op jit(solution)/shard_map/pallas_call | solution.py:590
  50.1 1.7 %copy.17 = bf16[128,1024]{1,0:T(8,128)(2,1)} copy(bf16[128,1024]{1,0:T(8,128)(2,1)} %get-tuple-element.4) | data formatting | bytes 524288
  51.7 1.6 %copy.18 = bf16[128,512]{1,0:T(8,128)(2,1)} copy(bf16[128,512]{1,0:T(8,128)(2,1)} %get-tuple-element.5) | data formatting | bytes 262144

commit v5 on v4

--- a/solution.py
+++ b/solution.py
@@ -479,9 +479,6 @@
 
     sent += pair_gather(h_all, x, m, local_width, head_parts, d_send, d_recv, head_part)
     scale = lax.rsqrt(squares[:, :1] * (1.0 / width) + EPSILON)
-    for j in range(2):
-        kv[0, j] = (kv_acc[j] * scale).astype(jnp.bfloat16)
-
     def kv_copy(d, part):
         return remote(
             kv.at[d - 1, part],
@@ -492,6 +489,7 @@
         )
 
     for part in range(2):
+        kv[0, part] = (kv_acc[part] * scale).astype(jnp.bfloat16)
 
         @pl.when(z + 1 < n)
         def _(part=part):

time: 54.2 us -> 54.2 us (level)
  no operation moved by 1% of the time
where the time goes in v5:
time: 54.2 us; the launch traced here: 53.3 us
  Pallas kernels  49.5 us (91%)
  local copies, waits for them, and re-layouts  3.24 us (6%)
  between operations  0.64 us (1%)
    pallas_call x1, Pallas kernels, aligned(): pl.pallas_call(functools.partial(layer_kernel, n, m), out_shape=(jax.Shap...  49.5 us
    unnamed x2, local copies, waits for them, and re-layouts  3.24 us

profile of v5, /device:TPU:30, one launch (start us, length us, event | category | flops | bytes accessed | tf_op | source)
XLA Modules:
  0.0 53.3 jit_solution(16942740452397840233)
XLA Ops:
  0.6 49.5 %shard_map.140 = (bf16[128,1024]{1,0:T(8,128)(2,1)}, bf16[128,512]{1,0:T(8,128)(2,1)}) custom-call(bf16[3,128,512]{2,1,0:T(8,128)(2,1)} %bitcast.6, f32[128,512]{1,0:T(8,128)} %filt_in.1, bf16[128,1024]{1,0:T(8,128)(2,1)} %residual_in.1, s32[1,512]{1,0:T(1,128)} %bitcast.8, f32[3,3,512]{2,1,0:T(4,128)} %taps_in.1, f32[1,512]{1,0:T(1,128)} %bitcast.9, ...), custom_call_target="tpu_custom_call" | custom-call | tf_op jit(solution)/shard_map/pallas_call | solution.py:588
  50.1 1.7 %copy.17 = bf16[128,1024]{1,0:T(8,128)(2,1)} copy(bf16[128,1024]{1,0:T(8,128)(2,1)} %get-tuple-element.4) | data formatting | bytes 524288
  51.8 1.6 %copy.18 = bf16[128,512]{1,0:T(8,128)(2,1)} copy(bf16[128,512]{1,0:T(8,128)(2,1)} %get-tuple-element.5) | data formatting | bytes 262144
